TPU v7x, 32 devices: a whole 2x2x4 slice. The times are simulated.
32 devices in a mesh: dp: 16 (over z, y, x), tensor: 2 (over core).
Axes of the slice: x: 2, y: 2, z: 4, core: 2. Of those that a mesh axis runs over, the one named last changes fastest.
Arguments:
- tokens: bfloat16 [128, 185, 768], P('dp'), may hold values from -6 to 6
- cotangent: bfloat16 [128, 185, 768], P('dp'), may hold values from -6 to 6
- caption_lengths: int32 [128], P('dp'), may hold values from 5 to 40
- item_counts: int32 [16], P('dp'), may hold values from 1 to 8, as said below
- w_qkv: bfloat16 [768, 3, 768], P(None, None, 'tensor'), may hold values from -0.21875 to 0.21875
- qv_bias: float32 [2, 768], P(None, 'tensor'), may hold values from -2 to 2
- w_out: bfloat16 [768, 768], P('tensor'), may hold values from -0.625 to 0.625
- out_bias: float32 [768], replicated, may hold values from -2 to 2
- w_up: bfloat16 [768, 3072], P(None, 'tensor'), may hold values from -0.21875 to 0.21875
- up_bias: float32 [3072], P('tensor'), may hold values from -3 to 3
- w_down: bfloat16 [3072, 768], P('tensor'), may hold values from -0.109375 to 0.109375
- down_bias: float32 [768], replicated, may hold values from -2 to 2
- ln_gains: float32 [2, 768], replicated, may hold values from 0.5 to 1.5
- ln_biases: float32 [2, 768], replicated, may hold values from -2 to 2
Outputs:
- output: bfloat16 [128, 185, 768], P('dp')
- grad_tokens: bfloat16 [128, 185, 768], P('dp')
- grad_qkv: float32 [768, 3, 768], P(None, None, 'tensor')
- grad_qv_bias: float32 [2, 768], P(None, 'tensor')
- grad_out: float32 [768, 768], P('tensor')
- grad_out_bias: float32 [768], replicated
- grad_up: float32 [768, 3072], P(None, 'tensor')
- grad_up_bias: float32 [3072], P('tensor')
- grad_down: float32 [3072, 768], P('tensor')
- grad_down_bias: float32 [768], replicated
- grad_ln_gains: float32 [2, 768], replicated
- grad_ln_biases: float32 [2, 768], replicated
Inputs may be any that keep to these rules, and one draw needn't show every extreme that they name: `item_counts`: item slots of a device at or beyond its count hold no item; some device has 8 live slots and some has 1.
All inputs are finite; a program needn't handle non-finite values.
Results may differ from a plain program's by a relative error of at most 0.013.
Values sent between devices are 32-bit elements; how exact they have to be, the bound alone decides.
No kernel may reach another device: no remote copies, remote signals or barrier semaphores. Data moves between devices by JAX's collectives and lax.ppermute only.
A program may use at most 192 MiB of HBM per device.

v0:
```python
import jax
import jax.numpy as jnp
from jax import lax
from jax.sharding import PartitionSpec as P

HEAD_DIM = 64
PATCHES = 144


layer_eps = 1e-05


def layer_norm(values, gain, shift):
    centred = values - jnp.mean(values, axis=-1, keepdims=True)
    variance = jnp.mean(centred * centred, axis=-1, keepdims=True)
    inverse = lax.rsqrt(variance + layer_eps)
    normal = centred * inverse
    return (normal * gain + shift, normal, inverse)


def norm_back(upstream, normal, inverse, gain):
    scaled = upstream * gain
    return inverse * (
        scaled
        - jnp.mean(scaled, axis=-1, keepdims=True)
        - normal * jnp.mean(scaled * normal, axis=-1, keepdims=True)
    )


def attention_scores(queries, keys_all, key_valid, score_scale):
    scores = (
        jnp.einsum("ishd,ithd->ihst", queries, keys_all, preferred_element_type=jnp.float32)
        * score_scale
    )
    return jnp.where(key_valid[:, None, None, :], scores, -1e30)


def on_device(
    tokens,
    cotangent,
    caption_lengths,
    item_counts,
    w_qkv,
    qv_bias,
    w_out,
    out_bias,
    w_up,
    up_bias,
    w_down,
    down_bias,
    ln_gains,
    ln_biases,
):
    batch_items, seq_len, model_width = tokens.shape
    local_width = w_qkv.shape[2]
    local_heads = local_width // HEAD_DIM
    total_rows = batch_items * seq_len
    score_scale = HEAD_DIM ** (-0.5)
    live_mask = (jnp.arange(batch_items, dtype=jnp.int32) < item_counts[0]).astype(jnp.float32)
    row_live = jnp.repeat(live_mask, seq_len)[:, None]
    key_valid = (
        jnp.arange(seq_len, dtype=jnp.int32)[None, :] < PATCHES + 1 + caption_lengths[:, None]
    )
    inputs = tokens.reshape(total_rows, model_width).astype(jnp.float32)
    normed, first_normal, first_inverse = layer_norm(inputs, ln_gains[0], ln_biases[0])
    normed_low = normed.astype(jnp.bfloat16)
    projected = jnp.einsum("rd,dce->rce", normed_low, w_qkv, preferred_element_type=jnp.float32)
    heads_shape = (batch_items, seq_len, local_heads, HEAD_DIM)
    queries = (projected[:, 0] + qv_bias[0]).astype(jnp.bfloat16).reshape(heads_shape)
    keys_all = projected[:, 1].astype(jnp.bfloat16).reshape(heads_shape)
    values_all = (projected[:, 2] + qv_bias[1]).astype(jnp.bfloat16).reshape(heads_shape)
    scores = attention_scores(queries, keys_all, key_valid, score_scale)
    row_peak = jnp.max(scores, axis=-1, keepdims=True)
    exp_total = jnp.sum(jnp.exp(scores - row_peak), axis=-1, keepdims=True)
    log_total = row_peak + jnp.log(exp_total)
    soft_weights = jnp.exp(scores - log_total)
    weights_low = soft_weights.astype(jnp.bfloat16)
    context = jnp.einsum(
        "ihst,ithd->ishd", weights_low, values_all, preferred_element_type=jnp.float32
    )
    context = context.reshape(total_rows, local_width).astype(jnp.bfloat16)
    attn_part = jnp.dot(context, w_out, preferred_element_type=jnp.float32)
    hidden = inputs + lax.psum(attn_part, "tensor") + out_bias
    second, second_normal, second_inverse = layer_norm(hidden, ln_gains[1], ln_biases[1])
    second_low = second.astype(jnp.bfloat16)
    upward = jnp.dot(second_low, w_up, preferred_element_type=jnp.float32) + up_bias
    active, gelu_pull = jax.vjp(lambda value: jax.nn.gelu(value, approximate=False), upward)
    active_low = active.astype(jnp.bfloat16)
    down_part = jnp.dot(active_low, w_down, preferred_element_type=jnp.float32)
    result = hidden + lax.psum(down_part, "tensor") + down_bias
    output = (result * row_live).astype(jnp.bfloat16).reshape(tokens.shape)
    upstream = cotangent.reshape(total_rows, model_width).astype(jnp.float32) * row_live
    upstream_low = upstream.astype(jnp.bfloat16)
    grad_down = jnp.einsum(
        "rf,rd->fd", active_low, upstream_low, preferred_element_type=jnp.float32
    )
    grad_down_bias = jnp.sum(upstream_low.astype(jnp.float32), axis=0)
    grad_active = jnp.einsum("rd,fd->rf", upstream_low, w_down, preferred_element_type=jnp.float32)
    grad_upward = gelu_pull(grad_active)[0].astype(jnp.bfloat16)
    grad_up = jnp.einsum("rd,rf->df", second_low, grad_upward, preferred_element_type=jnp.float32)
    grad_up_bias = jnp.sum(grad_upward.astype(jnp.float32), axis=0)
    second_part = jnp.einsum("rf,df->rd", grad_upward, w_up, preferred_element_type=jnp.float32)
    grad_second = lax.psum(second_part, "tensor")
    grad_hidden = upstream + norm_back(grad_second, second_normal, second_inverse, ln_gains[1])
    second_gain = jnp.sum(grad_second * second_normal, axis=0)
    second_shift = jnp.sum(grad_second, axis=0)
    grad_low = grad_hidden.astype(jnp.bfloat16)
    grad_out = jnp.einsum("re,rd->ed", context, grad_low, preferred_element_type=jnp.float32)
    grad_out_bias = jnp.sum(grad_low.astype(jnp.float32), axis=0)
    grad_context = jnp.einsum("rd,ed->re", grad_low, w_out, preferred_element_type=jnp.float32)
    grad_context = grad_context.astype(jnp.bfloat16).reshape(heads_shape)
    soft_again = jnp.exp(attention_scores(queries, keys_all, key_valid, score_scale) - log_total)
    again_low = soft_again.astype(jnp.bfloat16)
    grad_values = jnp.einsum(
        "ihst,ishd->ithd", again_low, grad_context, preferred_element_type=jnp.float32
    ).astype(jnp.bfloat16)
    grad_soft = jnp.einsum(
        "ishd,ithd->ihst", grad_context, values_all, preferred_element_type=jnp.float32
    )
    grad_scores = soft_again * (grad_soft - jnp.sum(soft_again * grad_soft, axis=-1, keepdims=True))
    grad_scores = grad_scores.astype(jnp.bfloat16)
    grad_queries = (
        jnp.einsum("ihst,ithd->ishd", grad_scores, keys_all, preferred_element_type=jnp.float32)
        * score_scale
    ).astype(jnp.bfloat16)
    grad_keys = (
        jnp.einsum("ihst,ishd->ithd", grad_scores, queries, preferred_element_type=jnp.float32)
        * score_scale
    ).astype(jnp.bfloat16)
    grad_proj = jnp.stack([grad_queries, grad_keys, grad_values], axis=2).reshape(
        total_rows, 3, local_width
    )
    grad_qkv = jnp.einsum("rd,rce->dce", normed_low, grad_proj, preferred_element_type=jnp.float32)
    grad_qv_bias = jnp.stack(
        [
            jnp.sum(grad_proj[:, 0].astype(jnp.float32), axis=0),
            jnp.sum(grad_proj[:, 2].astype(jnp.float32), axis=0),
        ]
    )
    normed_part = jnp.einsum("rce,dce->rd", grad_proj, w_qkv, preferred_element_type=jnp.float32)
    grad_normed = lax.psum(normed_part, "tensor")
    grad_inputs = grad_hidden + norm_back(grad_normed, first_normal, first_inverse, ln_gains[0])
    first_gain = jnp.sum(grad_normed * first_normal, axis=0)
    first_shift = jnp.sum(grad_normed, axis=0)
    (
        grad_qkv,
        grad_qv_bias,
        grad_out,
        grad_out_bias,
        first_gain,
        first_shift,
        grad_down,
        grad_down_bias,
        grad_up,
        grad_up_bias,
        second_gain,
        second_shift,
    ) = lax.psum(
        (
            grad_qkv,
            grad_qv_bias,
            grad_out,
            grad_out_bias,
            first_gain,
            first_shift,
            grad_down,
            grad_down_bias,
            grad_up,
            grad_up_bias,
            second_gain,
            second_shift,
        ),
        "dp",
    )
    grad_tokens = grad_inputs.astype(jnp.bfloat16).reshape(tokens.shape)
    grad_ln_gains = jnp.stack([first_gain, second_gain])
    grad_ln_biases = jnp.stack([first_shift, second_shift])
    return (
        output,
        grad_tokens,
        grad_qkv,
        grad_qv_bias,
        grad_out,
        grad_out_bias,
        grad_up,
        grad_up_bias,
        grad_down,
        grad_down_bias,
        grad_ln_gains,
        grad_ln_biases,
    )


def solution(mesh):
    return jax.shard_map(
        on_device,
        mesh=mesh,
        in_specs=(
            P("dp", None, None),
            P("dp", None, None),
            P("dp"),
            P("dp"),
            P(None, None, "tensor"),
            P(None, "tensor"),
            P("tensor", None),
            P(),
            P(None, "tensor"),
            P("tensor"),
            P("tensor", None),
            P(),
            P(),
            P(),
        ),
        out_specs=(
            P("dp", None, None),
            P("dp", None, None),
            P(None, None, "tensor"),
            P(None, "tensor"),
            P("tensor", None),
            P(),
            P(None, "tensor"),
            P("tensor"),
            P("tensor", None),
            P(),
            P(),
            P(),
        ),
        check_vma=False,
    )
```

profile of v0, /device:TPU:0, one launch (start us, length us, event | category | flops | bytes accessed | tf_op | source)
XLA Modules:
  0.0 728.7 jit_solution(15510239198412750371)
XLA Ops:
  15.1 5.1 reshape.171
  20.9 6.3 fusion.32
  33.1 4.8 squeeze.13
  71.6 5.0 fusion.38
  82.2 5.3 reshape.172
  87.4 21.0 %all-reduce.8.cloned.1.call-done = f32[1480,768]{1,0:T(8,128)} async-done(((f32[1480,768]{1,0:T(8,128)}), f32[1480,768]{1,0:T(8,128)}) %all-reduce.8.cloned.1.call-update) | async-done | bytes 4546576 | tf_op jit(solution)/shard_map/psum | solution.py:83
  113.4 25.3 %multiply_convert_fusion.1 = (bf16[1480,1536]{1,0:T(8,128)(2,1)}, f32[1480,1536]{1,0:T(8,128)}, f32[1480,1536]{1,0:T(8,128)}) fusion(f32[1536]{0:T(1024)S(1)} %copy-done.48, bf16[768,1536]{1,0:T(8,128)(2,1)S(1)} %copy-done, f32[1480,768]{1,0:T(8,128)S(1)} %get-tuple-element.93, f32[768]{0:T(1024)S(1)} %get-tuple-element.70, f32[768]{0:T(1024)S(1)} %get-tuple-element.108, ...), kind=kOutput, calls=%fused_computation.9 | convolution fusion | flops 3647477760 | bytes 29662784 | tf_op jit(solution)/shard_map/dot_general | solution.py:86
  138.8 10.5 %convert_reduce_fusion = (f32[1536]{0:T(1024)S(1)}, bf16[1480,1536]{1,0:T(8,128)(2,1)S(1)}) fusion(f32[1480,1536]{1,0:T(8,128)} %get-tuple-element.91, f32[1480,1536]{1,0:T(8,128)} %get-tuple-element.98, bf16[1536,768]{1,0:T(8,128)(2,1)S(1)} %copy-done.45, f32[1480,768]{1,0:T(8,128)S(1)} %bitcast.55, f32[1480]{0:T(1024)S(1)} %mul.180), kind=kOutput, calls=%fused_computation.7 | convolution fusion | flops 3530402304 | bytes 29650720 | tf_op jit(solution)/shard_map/rd,fd->rf/dot_general | solution.py:98
  151.3 5.4 fusion.40
  158.4 8.1 %fusion.39 = f32[1480,768]{1,0:T(8,128)} fusion(bf16[1480,1536]{1,0:T(8,128)(2,1)} %get-tuple-element.90, bf16[1536,768]{1,0:T(8,128)(2,1)S(1)} %copy-done.46), kind=kOutput, calls=%fused_computation.108 | convolution fusion | flops 3491758080 | bytes 11452416 | tf_op jit(solution)/shard_map/dot_general | solution.py:89
  166.5 20.4 %all-reduce.10.cloned.1.call-done = f32[1480,768]{1,0:T(8,128)} async-done(((f32[1480,768]{1,0:T(8,128)}), f32[1480,768]{1,0:T(8,128)}) %all-reduce.10.cloned.1.call-update) | async-done | bytes 4546576 | tf_op jit(solution)/shard_map/psum | solution.py:103
  186.9 4.9 multiply_reduce_fusion.1
  191.9 5.2 convert_reduce_fusion.2
  208.3 7.9 %convert_reduce_fusion.3 = (f32[6,64]{1,0:T(8,128)S(1)}, bf16[8,185,6,64]{1,3,2,0:T(8,128)(2,1)}) fusion(bf16[8,185,6,64]{1,3,2,0:T(8,128)(2,1)} %copy.111, f32[8,6,185,185]{2,3,1,0:T(8,128)} %copy-done.2, f32[8,6,185]{2,1,0:T(8,128)S(1)} %copy-done.25, pred[8,185]{1,0:T(8,128)(4,1)S(1)} %iota_compare_fusion), kind=kOutput, calls=%fused_computation.47 | convolution fusion | flops 218554176 | bytes 8883016 | tf_op jit(solution)/shard_map/ihst,ishd->ithd/dot_general | solution.py:114
  216.2 6.1 multiply_reduce_fusion
  257.5 4.8 convolution_bitcast_fusion
  262.9 10.5 %fusion.28 = f32[1536,768]{1,0:T(8,128)} fusion(bf16[1480,1536]{1,0:T(8,128)(2,1)} %get-tuple-element.90, f32[1480,768]{1,0:T(8,128)} %reshape.172, f32[1480]{0:T(1024)S(1)} %mul.180), kind=kOutput, calls=%fused_computation.100 | convolution fusion | flops 3494031360 | bytes 13817632 | tf_op jit(solution)/shard_map/rf,rd->fd/dot_general | solution.py:94
  273.4 12.3 %fusion.34 = f32[768,1536]{1,0:T(8,128)} fusion(bf16[1480,1536]{1,0:T(8,128)(2,1)} %copy-done.50, f32[1480,768]{1,0:T(8,128)} %copy-done.3, f32[768]{0:T(1024)S(1)} %copy-done.41, f32[768]{0:T(1024)S(1)} %get-tuple-element.108, f32[1480]{0:T(1024)S(1)} %add_rsqrt_fusion, f32[1480]{0:T(1024)S(1)} %broadcast_multiply_fusion.4), kind=kOutput, calls=%fused_computation.104 | convolution fusion | flops 3497441280 | bytes 13829696 | tf_op jit(solution)/shard_map/rd,rf->df/dot_general | solution.py:100
  287.9 5.7 fusion.30
  296.7 7.2 all-reduce.14.cloned.1.call-done
  303.9 4.9 multiply_reduce_fusion.2
  308.9 5.5 add_convert_fusion.1
  329.9 82.3 %all-reduce = (f32[2,384]{1,0:T(2,128)}, f32[768]{0:T(1024)}, f32[1536]{0:T(1024)}, f32[768]{0:T(1024)}, f32[1,768]{1,0:T(1,128)S(1)}, /*index=5*/f32[1,768]{1,0...) all-reduce(f32[2,384]{1,0:T(2,128)S(1)} %pad_maximum_fusion.2, ...), channel_id=1, replica_groups=mesh['dp'=16,'tensor'=2] {'dp'}, use_global_device_ids=true, to_apply=%region_18.19 | all-reduce | flops 6912 | bytes 55296 | tf_op jit(solution)/shard_map/psum | solution.py:158
  413.3 297.8 %all-reduce.12.cloned.1.call-done = (f32[768,3,384]{2,0,1:T(8,128)}, f32[384,768]{1,0:T(8,128)}, f32[768,1536]{1,0:T(8,128)}, f32[1536,768]{1,0:T(8,128)}) async-done(((f32[768,3,384]{2,0,1:T(8,128)}, f32[384,768]{1,0:T(8,128)}, f32[768,1536]{1,0:T(8,128)}, f32[1536,768]{1,0:T(8,128)}), (f32[768,3,384]{2,0,1:T(8,128)}, f32[384,768]{1,0:T(8,128)}, f32[768,1536]{1,0:T(8,128)}, ...) | async-done | bytes 14155792 | tf_op jit(solution)/shard_map/psum | solution.py:158
  (220 shorter events, 141.0 us)
Async XLA Ops:
  7.2 106.2 %copy-start = (bf16[768,1536]{1,0:T(8,128)(2,1)S(1)}, bf16[768,1536]{1,0:T(8,128)(2,1)}, u32[]{:S(2)}) copy-start(bf16[768,1536]{1,0:T(8,128)(2,1)} %param.22) | copy-start | bytes 7077892
  7.2 101.2 %all-reduce.8.cloned.1.call-start = ((), (), s32[]{:S(2)}) async-start(), calls=%async_computation | async-start | bytes 9093120 | tf_op jit(solution)/shard_map/psum | solution.py:83
  9.6 10.8 %copy-start.28 = (f32[1480]{0:T(1024)}, f32[1480]{0:T(1024)S(1)}, u32[]{:S(2)}) copy-start(f32[1480]{0:T(1024)S(1)} %div.27) | copy-start | bytes 17764
  20.4 93.0 %copy-start.40 = (f32[768]{0:T(1024)}, f32[768]{0:T(1024)S(1)}, u32[]{:S(2)}) copy-start(f32[768]{0:T(1024)S(1)} %get-tuple-element.70) | copy-start | bytes 9220
  76.6 110.3 %all-reduce.10.cloned.1.call-start = ((), (), s32[]{:S(2)}) async-start(), calls=%async_computation.1 | async-start | bytes 9093120 | tf_op jit(solution)/shard_map/psum | solution.py:103
  82.2 26.2 %copy-start.36 = (f32[768]{0:T(1024)S(1)}, f32[768]{0:T(1024)}, u32[]{:S(2)}) copy-start(f32[768]{0:T(1024)} %param.21) | copy-start | bytes 9220
  112.6 26.1 %copy-start.3 = (f32[1480,768]{1,0:T(8,128)}, f32[1480,768]{1,0:T(8,128)S(1)}, u32[]{:S(2)}) copy-start(f32[1480,768]{1,0:T(8,128)S(1)} %get-tuple-element.93) | copy-start | bytes 13639684
  112.7 26.1 %slice-start.7 = ((s8[4546560]{0:T(1024)(128)(4,1)}), s8[4194304]{0:T(1024)(128)(4,1)S(1)}, s32[]{:S(2)}) async-start(s8[4546560]{0:T(1024)(128)(4,1)} %bitcast.54), calls=%async_computation.11 | async-start | bytes 8388608
  113.4 25.4 %slice-start.8 = ((s8[4546560]{0:T(1024)(128)(4,1)}), s8[352256]{0:T(1024)(128)(4,1)S(1)}, s32[]{:S(2)}) async-start(s8[4546560]{0:T(1024)(128)(4,1)} %bitcast.54), calls=%async_computation.12 | async-start | bytes 704512
  113.4 25.3 %copy-start.45 = (bf16[1536,768]{1,0:T(8,128)(2,1)S(1)}, bf16[1536,768]{1,0:T(8,128)(2,1)}, u32[]{:S(2)}) copy-start(bf16[1536,768]{1,0:T(8,128)(2,1)} %param.24) | copy-start | bytes 7077892
  156.7 147.2 %all-reduce.14.cloned.1.call-start = ((), (), s32[]{:S(2)}) async-start(), calls=%async_computation.3 | async-start | bytes 18186240 | tf_op jit(solution)/shard_map/psum | solution.py:90
  200.6 7.7 %copy-start.25 = (f32[8,6,185]{2,1,0:T(8,128)S(1)}, f32[8,6,185]{2,1,0:T(8,128)}, u32[]{:S(2)}) copy-start(f32[8,6,185]{2,1,0:T(8,128)} %copy-done.24) | copy-start | bytes 106564
  208.3 7.9 %copy-start.18 = (bf16[8,185,6,64]{1,0,3,2:T(8,128)(2,1)S(1)}, bf16[8,185,6,64]{1,0,3,2:T(8,128)(2,1)}, u32[]{:S(2)}) copy-start(bf16[8,185,6,64]{1,0,3,2:T(8,128)(2,1)} %copy-done.17) | copy-start | bytes 3409924
  208.3 7.9 %copy-start.19 = (bf16[8,185,6,64]{1,3,2,0:T(8,128)(2,1)S(1)}, bf16[8,185,6,64]{1,3,2,0:T(8,128)(2,1)}, u32[]{:S(2)}) copy-start(bf16[8,185,6,64]{1,3,2,0:T(8,128)(2,1)} %copy.111) | copy-start | bytes 3409924
  208.3 14.0 %slice-start = ((s8[9437184]{0:T(1024)(128)(4,1)}), s8[4194304]{0:T(1024)(128)(4,1)S(1)}, s32[]{:S(2)}) async-start(s8[9437184]{0:T(1024)(128)(4,1)} %bitcast.48), calls=%async_computation.4 | async-start | bytes 8388608
  208.3 14.0 %slice-start.1 = ((s8[9437184]{0:T(1024)(128)(4,1)}), s8[4194304]{0:T(1024)(128)(4,1)S(1)}, s32[]{:S(2)}) async-start(s8[9437184]{0:T(1024)(128)(4,1)} %bitcast.48), calls=%async_computation.5 | async-start | bytes 8388608
  238.7 9.4 %copy-start.13 = (bf16[8,185,6,64]{1,3,2,0:T(8,128)(2,1)S(1)}, bf16[8,185,6,64]{1,3,2,0:T(8,128)(2,1)}, u32[]{:S(2)}) copy-start(bf16[8,185,6,64]{1,3,2,0:T(8,128)(2,1)} %get-tuple-element.104) | copy-start | bytes 3409924
  262.4 11.0 %copy-start.41 = (f32[768]{0:T(1024)S(1)}, f32[768]{0:T(1024)}, u32[]{:S(2)}) copy-start(f32[768]{0:T(1024)} %copy-done.40) | copy-start | bytes 9220
  262.4 448.8 %all-reduce.12.cloned.1.call-start = ((), (), s32[]{:S(2)}) async-start(), calls=%async_computation.2 | async-start | bytes 28311552 | tf_op jit(solution)/shard_map/psum | solution.py:158
  262.8 22.8 %slice-start.5 = ((s8[4546560]{0:T(1024)(128)(4,1)}), s8[4194304]{0:T(1024)(128)(4,1)S(1)}, s32[]{:S(2)}) async-start(s8[4546560]{0:T(1024)(128)(4,1)} %bitcast.52), calls=%async_computation.9 | async-start | bytes 8388608
  262.8 25.0 %slice-start.3 = ((s8[4546560]{0:T(1024)(128)(4,1)}), s8[4194304]{0:T(1024)(128)(4,1)S(1)}, s32[]{:S(2)}) async-start(s8[4546560]{0:T(1024)(128)(4,1)} %bitcast.50), calls=%async_computation.7 | async-start | bytes 8388608
  273.4 12.3 %slice-start.6 = ((s8[4546560]{0:T(1024)(128)(4,1)}), s8[352256]{0:T(1024)(128)(4,1)S(1)}, s32[]{:S(2)}) async-start(s8[4546560]{0:T(1024)(128)(4,1)} %bitcast.52), calls=%async_computation.10 | async-start | bytes 704512
  273.4 12.3 %copy-start.16 = (bf16[1480,384]{0,1:T(8,128)(2,1)S(1)}, bf16[1480,384]{0,1:T(8,128)(2,1)}, u32[]{:S(2)}) copy-start(bf16[1480,384]{0,1:T(8,128)(2,1)} %copy-done.15) | copy-start | bytes 3409924
  273.4 14.5 %slice-start.4 = ((s8[4546560]{0:T(1024)(128)(4,1)}), s8[352256]{0:T(1024)(128)(4,1)S(1)}, s32[]{:S(2)}) async-start(s8[4546560]{0:T(1024)(128)(4,1)} %bitcast.50), calls=%async_computation.8 | async-start | bytes 704512
  (44 other events, 146.6 us)
Sparse Core Ops, SparseCore 0:
  76.8 31.5 all-reduce.7
  156.8 30.0 all-reduce.9
  262.5 41.3 all-reduce.13
  311.3 399.7 all-reduce.11
where the time goes:
time: 733 us; the launch traced here: 729 us
  waiting for transfers between devices  346 us (47%)
  matrix products  121 us (17%)
  local copies, waits for them, and re-layouts  119 us (16%)
  blocking collectives  82.3 us (11%)
  other arithmetic  43.5 us (6%)
  between operations  15.5 us (2%)
    psum x1, waiting for transfers between devices, on_device(): lax.psum((grad_qkv, grad_qv_bias, grad_out, grad_out_bias, first_gain, fi...  298 us
    psum x1, blocking collectives, on_device(): lax.psum((grad_qkv, grad_qv_bias, grad_out, grad_out_bias, first_gain, fi...  82.3 us
    unnamed x136, local copies, waits for them, and re-layouts  29.5 us
    dot_general x1, matrix products, on_device(): jnp.dot(second_low, w_up, preferred_element_type=jnp.float32) + up_bias  25.3 us
    another operation x7, local copies, waits for them, and re-layouts, on_device(): jnp.stack([grad_queries, grad_keys, grad_values], axis=2)  25.1 us
    psum x1, waiting for transfers between devices, on_device(): hidden = inputs + lax.psum(attn_part, 'tensor') + out_bias  21 us
    psum x1, waiting for transfers between devices, on_device(): grad_second = lax.psum(second_part, 'tensor')  20.4 us
  transfers between devices with their start and end apart: 4, of which 4 were waited for; matrix products, arithmetic and copies ran while one was open for 10% of the time, Pallas kernels for 0%

commit v1 on v0

v1 whole, which is shorter than its diff:
```python
import jax
import jax.numpy as jnp
from jax import lax
from jax.experimental import pallas as pl
from jax.experimental.pallas import tpu as pltpu
from jax.sharding import PartitionSpec as P

HEAD_DIM = 64
PATCHES = 144
EPS = 1e-05
VMEM_LIMIT = 56 * 1024 * 1024
F32 = jnp.float32
BF16 = jnp.bfloat16


def mm(a, b, da=1, db=0):
    return lax.dot_general(a, b, (((da,), (db,)), ((), ())), preferred_element_type=F32)


def whole(shape):
    return pl.BlockSpec(shape, lambda *_: (0,) * len(shape))


def anywhere():
    return pl.BlockSpec(memory_space=pl.ANY)


def smem():
    return pl.BlockSpec(memory_space=pltpu.SMEM)


def call(body, grid, ins, in_specs, outs, out_specs, scratch=(), aliases=None, after=(), flops=0):
    n_in, n_after = len(ins), len(after)

    def kernel(*refs):
        body(*refs[:n_in], *refs[n_in + n_after :])

    size = sum(v.size * v.dtype.itemsize for v in ins) + sum(v.size * v.dtype.itemsize for v in outs)
    return pl.pallas_call(
        kernel,
        grid=grid,
        in_specs=list(in_specs) + [anywhere()] * n_after,
        out_specs=list(out_specs),
        out_shape=list(outs),
        scratch_shapes=list(scratch),
        input_output_aliases=aliases or {},
        compiler_params=pltpu.CompilerParams(vmem_limit_bytes=VMEM_LIMIT),
        cost_estimate=pl.CostEstimate(flops=int(flops), bytes_accessed=int(size), transcendentals=0),
    )(*ins, *after)


def sds(shape, dtype):
    return jax.ShapeDtypeStruct(shape, dtype)


def normed(v):
    centred = v - jnp.mean(v, axis=-1, keepdims=True)
    inverse = lax.rsqrt(jnp.mean(centred * centred, axis=-1, keepdims=True) + EPS)
    return centred * inverse, inverse


def norm_back(e, n, inverse, gain):
    eg = e * gain
    return inverse * (
        eg - jnp.mean(eg, axis=-1, keepdims=True) - n * jnp.mean(eg * n, axis=-1, keepdims=True)
    )


def colsum(v):
    return jnp.sum(v, axis=0, keepdims=True)


def on_device(
    tokens,
    cotangent,
    caption_lengths,
    item_counts,
    w_qkv,
    qv_bias,
    w_out,
    out_bias,
    w_up,
    up_bias,
    w_down,
    down_bias,
    ln_gains,
    ln_biases,
):
    items, seq, D = tokens.shape
    W = w_qkv.shape[2]
    FL = w_up.shape[1]
    pairs = W // 128
    heads = W // HEAD_DIM
    SP = -(-seq // 64) * 64
    R = items * SP
    IB = 2
    BR = IB * SP
    halves = 2
    steps = items // IB // halves
    total_steps = items // IB
    scale = HEAD_DIM ** (-0.5)

    wq = w_qkv.reshape(D, 3 * W)
    bias3 = jnp.concatenate([qv_bias[0], jnp.zeros((W,), F32), qv_bias[1]]).reshape(1, 3 * W)
    g1, g2 = ln_gains[0:1], ln_gains[1:2]
    b1, b2 = ln_biases[0:1], ln_biases[1:2]
    out_b = out_bias.reshape(1, D)
    down_b = down_bias.reshape(1, D)
    up_b = up_bias.reshape(1, FL)

    def padded(ref, i, scratch):
        rows = pl.ds(i * SP, seq)
        scratch[pl.ds(i * SP + seq // 8 * 8, SP - seq // 8 * 8), :] = jnp.zeros(
            (SP - seq // 8 * 8, D), F32
        )
        scratch[rows, :] = ref[i].astype(F32)

    def attn_fwd(off):
        def body(len_ref, tok_ref, wq_ref, b3_ref, g_ref, b_ref, wo_ref, *rest):
            part_ref, a_ref, qkv_ref, pr_ref, ctx_ref, xs = rest[-6:]
            step = pl.program_id(0)
            for i in range(IB):
                padded(tok_ref, i, xs)
            n, _ = normed(xs[...])
            a = (n * g_ref[...] + b_ref[...]).astype(BF16)
            a_ref[...] = a
            qkv_ref[...] = (mm(a, wq_ref[...]) + b3_ref[...]).astype(BF16)
            lane = lax.broadcasted_iota(jnp.int32, (SP, 128), 1)
            key_at = lax.broadcasted_iota(jnp.int32, (SP, SP), 0)
            zero = jnp.zeros((SP, 128), BF16)
            for i in range(IB):
                limit = PATCHES + 1 + len_ref[(step + off) * IB + i]
                valid = key_at < limit
                rows = pl.ds(i * SP, SP)
                for j in range(pairs):
                    q = qkv_ref[rows, pl.ds(j * 128, 128)] * jnp.asarray(scale, BF16)
                    k = qkv_ref[rows, pl.ds(W + j * 128, 128)]
                    v = qkv_ref[rows, pl.ds(2 * W + j * 128, 128)]
                    ctx = None
                    for s in range(2):
                        mine = (lane < 64) if s == 0 else (lane >= 64)
                        st = mm(k, jnp.where(mine, q, zero), 1, 1)
                        st = jnp.where(valid, st, -1e30)
                        e = jnp.exp(st - jnp.max(st, axis=0, keepdims=True))
                        pr = (e * (1.0 / jnp.sum(e, axis=0, keepdims=True))).astype(BF16)
                        pr_ref[i, 2 * j + s] = pr
                        c = mm(pr, jnp.where(mine, v, zero), 0, 0)
                        ctx = c if ctx is None else ctx + c
                    ctx_ref[rows, pl.ds(j * 128, 128)] = ctx.astype(BF16)
            part_ref[...] = mm(ctx_ref[...], wo_ref[...])

        return body

    kept = None
    parts = []
    for half in range(halves):
        off = half * steps
        row = lambda t, o=off: (t + o, 0)
        ins = [caption_lengths, tokens, wq, bias3, g1, b1, w_out]
        specs = [
            smem(),
            pl.BlockSpec((IB, seq, D), lambda t, o=off: (t + o, 0, 0)),
            whole((D, 3 * W)),
            whole((1, 3 * W)),
            whole((1, D)),
            whole((1, D)),
            whole((W, D)),
        ]
        outs = [
            sds((R // halves, D), F32),
            sds((R, D), BF16),
            sds((R, 3 * W), BF16),
            sds((items, heads, SP, SP), BF16),
            sds((R, W), BF16),
        ]
        out_specs = [
            pl.BlockSpec((BR, D), lambda t: (t, 0)),
            pl.BlockSpec((BR, D), row),
            pl.BlockSpec((BR, 3 * W), row),
            pl.BlockSpec((IB, heads, SP, SP), lambda t, o=off: (t + o, 0, 0, 0)),
            pl.BlockSpec((BR, W), row),
        ]
        aliases = {}
        if kept is not None:
            aliases = {len(ins) + n: 1 + n for n in range(4)}
            ins += kept
            specs += [anywhere()] * 4
        res = call(
            attn_fwd(off),
            (steps,),
            ins,
            specs,
            outs,
            out_specs,
            [pltpu.VMEM((BR, D), F32)],
            aliases,
            flops=R * D * W * 4,
        )
        parts.append(res[0])
        kept = list(res[1:])
    a_all, qkv, prs, ctx_all = kept

    swap = [(0, 1), (1, 0)]

    def other(v):
        return lax.ppermute(v, "tensor", swap)

    got = [other(p) for p in parts]

    def second(off):
        def body(cnt_ref, tok_ref, cot_ref, p_ref, r_ref, ob_ref, g_ref, b_ref, *rest):
            h_ref, c_ref, ct_ref, dy_ref, sum_ref, xs = rest[-6:]
            step = pl.program_id(0)
            for i in range(IB):
                padded(tok_ref, i, xs)
            h = xs[...] + (p_ref[...] + r_ref[...]) + ob_ref[...]
            h_ref[...] = h.astype(BF16)
            n, _ = normed(h)
            c = (n * g_ref[...] + b_ref[...]).astype(BF16)
            c_ref[...] = c
            ct_ref[...] = c.T
            for i in range(IB):
                padded(cot_ref, i, xs)
            item = (step + off) * IB + lax.broadcasted_iota(jnp.int32, (BR, D), 0) // SP
            dy = jnp.where(item < cnt_ref[0], xs[...], 0.0)
            dy_ref[...] = dy.astype(BF16)
            sum_ref[0] = colsum(dy)

        return body

    kept = None
    for half in range(halves):
        off = half * steps
        row = lambda t, o=off: (t + o, 0)
        tok_spec = pl.BlockSpec((IB, seq, D), lambda t, o=off: (t + o, 0, 0))
        ins = [item_counts, tokens, cotangent, parts[half], got[half], out_b, g2, b2]
        specs = [
            smem(),
            tok_spec,
            tok_spec,
            pl.BlockSpec((BR, D), lambda t: (t, 0)),
            pl.BlockSpec((BR, D), lambda t: (t, 0)),
            whole((1, D)),
            whole((1, D)),
            whole((1, D)),
        ]
        outs = [
            sds((R, D), BF16),
            sds((R, D), BF16),
            sds((D, R), BF16),
            sds((R, D), BF16),
            sds((total_steps, 1, D), F32),
        ]
        out_specs = [
            pl.BlockSpec((BR, D), row),
            pl.BlockSpec((BR, D), row),
            pl.BlockSpec((D, BR), lambda t, o=off: (0, t + o)),
            pl.BlockSpec((BR, D), row),
            pl.BlockSpec((1, 1, D), lambda t, o=off: (t + o, 0, 0)),
        ]
        aliases = {}
        if kept is not None:
            aliases = {len(ins) + n: n for n in range(5)}
            ins += kept
            specs += [anywhere()] * 5
        kept = list(
            call(second(off), (steps,), ins, specs, outs, out_specs, [pltpu.VMEM((BR, D), F32)], aliases)
        )
    h_all, c_all, ct_all, dy_all, dy_sums = kept

    FC = 384 if FL % 384 == 0 else FL
    RB = R // 2
    SB = 256

    def ffn(f):
        def body(c_ref, ct_ref, dy_ref, wu_ref, ub_ref, wd_ref, *rest):
            gd_ref, gu_ref, sum_ref, r_ref, du_ref = rest[-5:]
            step = pl.program_id(0)
            total = None
            for s in range(RB // SB):
                rows = pl.ds(s * SB, SB)
                u = mm(c_ref[rows, :], wu_ref[...]) + ub_ref[...]
                half_erf = 0.5 + 0.5 * lax.erf(u * (0.5**0.5))
                r_ref[rows, :] = (u * half_erf).astype(BF16)
                slope = half_erf + u * (jnp.exp(-0.5 * u * u) * 0.3989422804014327)
                dr = mm(dy_ref[rows, :], wd_ref[...], 1, 1)
                du = (dr * slope).astype(BF16)
                du_ref[rows, :] = du
                t = colsum(du.astype(F32))
                total = t if total is None else total + t
            gd = mm(r_ref[...], dy_ref[...], 0, 0)
            gu = mm(ct_ref[...], du_ref[...])

            @pl.when(step == 0)
            def _():
                gd_ref[...] = gd
                gu_ref[...] = gu
                sum_ref[...] = total

            @pl.when(step > 0)
            def _():
                gd_ref[...] += gd
                gu_ref[...] += gu
                sum_ref[...] += total

        return body

    kept = None
    gds, gus, up_sums = [], [], []
    for f in range(FL // FC):
        ins = [c_all, ct_all, dy_all, w_up, up_b, w_down]
        specs = [
            pl.BlockSpec((RB, D), lambda t: (t, 0)),
            pl.BlockSpec((D, RB), lambda t: (0, t)),
            pl.BlockSpec((RB, D), lambda t: (t, 0)),
            pl.BlockSpec((D, FC), lambda t, f=f: (0, f)),
            pl.BlockSpec((1, FC), lambda t, f=f: (0, f)),
            pl.BlockSpec((FC, D), lambda t, f=f: (f, 0)),
        ]
        outs = [
            sds((FC, D), F32),
            sds((D, FC), F32),
            sds((1, FC), F32),
            sds((R, FL), BF16),
            sds((R, FL), BF16),
        ]
        out_specs = [
            whole((FC, D)),
            whole((D, FC)),
            whole((1, FC)),
            pl.BlockSpec((RB, FC), lambda t, f=f: (t, f)),
            pl.BlockSpec((RB, FC), lambda t, f=f: (t, f)),
        ]
        aliases = {}
        if kept is not None:
            aliases = {len(ins) + n: 3 + n for n in range(2)}
            ins += kept
            specs += [anywhere()] * 2
        gd, gu, us, r_all, du_all = call(
            ffn(f), (R // RB,), ins, specs, outs, out_specs, (), aliases, flops=8 * R * D * FC
        )
        kept = [r_all, du_all]
        gds.append(gd)
        gus.append(gu)
        up_sums.append(us)

    def dc_body(du_ref, w_ref, o_ref):
        o_ref[...] = mm(du_ref[...], w_ref[...], 1, 1)

    def y_body(r_ref, w_ref, o_ref):
        o_ref[...] = mm(r_ref[...], w_ref[...])

    MB = R // 4
    (dc_part,) = call(
        dc_body,
        (R // MB,),
        [du_all, w_up],
        [pl.BlockSpec((MB, FL), lambda t: (t, 0)), whole((D, FL))],
        [sds((R, D), F32)],
        [pl.BlockSpec((MB, D), lambda t: (t, 0))],
        flops=2 * R * D * FL,
    )
    dc_got = other(dc_part)
    (y_part,) = call(
        y_body,
        (R // MB,),
        [r_all, w_down],
        [pl.BlockSpec((MB, FL), lambda t: (t, 0)), whole((FL, D))],
        [sds((R, D), F32)],
        [pl.BlockSpec((MB, D), lambda t: (t, 0))],
        flops=2 * R * D * FL,
        after=(dc_part,),
    )
    y_got = other(y_part)

    def back2_body(p_ref, r_ref, h_ref, dy_ref, ctx_ref, wo_ref, g_ref, dh_ref, dctx_ref, go_ref, sum_ref):
        step = pl.program_id(0)
        e = p_ref[...] + r_ref[...]
        n, inverse = normed(h_ref[...].astype(F32))
        dh = dy_ref[...].astype(F32) + norm_back(e, n, inverse, g_ref[...])
        dhr = dh.astype(BF16)
        dh_ref[...] = dhr
        dctx_ref[...] = mm(dhr, wo_ref[...], 1, 1).astype(BF16)
        sum_ref[0, 0:1] = colsum(e * n)
        sum_ref[0, 1:2] = colsum(e)
        sum_ref[0, 2:3] = colsum(dhr.astype(F32))
        go = mm(ctx_ref[...], dhr, 0, 0)

        @pl.when(step == 0)
        def _():
            go_ref[...] = go

        @pl.when(step > 0)
        def _():
            go_ref[...] += go

    rowD = pl.BlockSpec((BR, D), lambda t: (t, 0))
    rowW = pl.BlockSpec((BR, W), lambda t: (t, 0))
    row3 = pl.BlockSpec((BR, 3 * W), lambda t: (t, 0))
    dh_all, dctx_all, go, back2_sums = call(
        back2_body,
        (total_steps,),
        [dc_part, dc_got, h_all, dy_all, ctx_all, w_out, g2],
        [rowD, rowD, rowD, rowD, rowW, whole((W, D)), whole((1, D))],
        [sds((R, D), BF16), sds((R, W), BF16), sds((W, D), F32), sds((total_steps, 3, D), F32)],
        [rowD, rowW, whole((W, D)), pl.BlockSpec((1, 3, D), lambda t: (t, 0, 0))],
        after=(y_part,),
        flops=4 * R * D * W,
    )

    def attn_back_body(pr_ref, qkv_ref, dctx_ref, wq_ref, dqkv_ref, da_ref, sum_ref):
        lane = lax.broadcasted_iota(jnp.int32, (SP, 128), 1)
        zero = jnp.zeros((SP, 128), BF16)
        for i in range(IB):
            rows = pl.ds(i * SP, SP)
            for j in range(pairs):
                q = qkv_ref[rows, pl.ds(j * 128, 128)] * jnp.asarray(scale, BF16)
                k = qkv_ref[rows, pl.ds(W + j * 128, 128)]
                v = qkv_ref[rows, pl.ds(2 * W + j * 128, 128)]
                dctx = dctx_ref[rows, pl.ds(j * 128, 128)]
                dq = dk = dv = None
                for s in range(2):
                    mine = (lane < 64) if s == 0 else (lane >= 64)
                    pr = pr_ref[i, 2 * j + s]
                    dc = jnp.where(mine, dctx, zero)
                    dv_h = mm(pr, dc)
                    dp = mm(v, dc, 1, 1)
                    p = pr.astype(F32)
                    pdp = p * dp
                    ds = (pdp - p * jnp.sum(pdp, axis=0, keepdims=True)).astype(BF16)
                    dk_h = mm(ds, jnp.where(mine, q, zero))
                    dq_h = mm(ds, jnp.where(mine, k, zero), 0, 0)
                    dq = dq_h if dq is None else dq + dq_h
                    dk = dk_h if dk is None else dk + dk_h
                    dv = dv_h if dv is None else dv + dv_h
                dqkv_ref[rows, pl.ds(j * 128, 128)] = (dq * scale).astype(BF16)
                dqkv_ref[rows, pl.ds(W + j * 128, 128)] = dk.astype(BF16)
                dqkv_ref[rows, pl.ds(2 * W + j * 128, 128)] = dv.astype(BF16)
        dqkv = dqkv_ref[...]
        da_ref[...] = mm(dqkv, wq_ref[...], 1, 1)
        sum_ref[0] = colsum(dqkv.astype(F32))

    dqkv, da_part, qkv_sums = call(
        attn_back_body,
        (total_steps,),
        [prs, qkv, dctx_all, wq],
        [
            pl.BlockSpec((IB, heads, SP, SP), lambda t: (t, 0, 0, 0)),
            row3,
            rowW,
            whole((D, 3 * W)),
        ],
        [sds((R, 3 * W), BF16), sds((R, D), F32), sds((total_steps, 1, 3 * W), F32)],
        [row3, rowD, pl.BlockSpec((1, 1, 3 * W), lambda t: (t, 0, 0))],
        flops=6 * R * D * W,
    )
    da_got = other(da_part)

    def gqkv_body(a_ref, dqkv_ref, o_ref, at):
        @pl.when(pl.program_id(0) == 0)
        def _():
            at[...] = a_ref[...].T

        o_ref[0] = mm(at[...], dqkv_ref[...])

    (gqkv,) = call(
        gqkv_body,
        (3,),
        [a_all, dqkv],
        [whole((R, D)), pl.BlockSpec((R, W), lambda t: (0, t))],
        [sds((3, D, W), F32)],
        [pl.BlockSpec((1, D, W), lambda t: (t, 0, 0))],
        [pltpu.VMEM((D, R), BF16)],
        flops=6 * R * D * W,
        after=(da_part,),
    )

    def back1_body(tok_ref, p_ref, r_ref, dh_ref, g_ref, o_ref, sum_ref, xs):
        for i in range(IB):
            padded(tok_ref, i, xs)
        e = p_ref[...] + r_ref[...]
        n, inverse = normed(xs[...])
        dx = dh_ref[...].astype(F32) + norm_back(e, n, inverse, g_ref[...])
        xs[...] = dx
        for i in range(IB):
            o_ref[i] = xs[pl.ds(i * SP, seq), :].astype(BF16)
        sum_ref[0, 0:1] = colsum(e * n)
        sum_ref[0, 1:2] = colsum(e)

    tok_spec = pl.BlockSpec((IB, seq, D), lambda t: (t, 0, 0))
    grad_tokens, back1_sums = call(
        back1_body,
        (total_steps,),
        [tokens, da_part, da_got, dh_all, g1],
        [tok_spec, rowD, rowD, rowD, whole((1, D))],
        [sds(tokens.shape, BF16), sds((total_steps, 2, D), F32)],
        [tok_spec, pl.BlockSpec((1, 2, D), lambda t: (t, 0, 0))],
        [pltpu.VMEM((BR, D), F32)],
        after=(gqkv,),
    )

    def out_body(cnt_ref, h_ref, p_ref, r_ref, b_ref, o_ref, xs):
        step = pl.program_id(0)
        y = h_ref[...].astype(F32) + (p_ref[...] + r_ref[...]) + b_ref[...]
        item = step * IB + lax.broadcasted_iota(jnp.int32, (BR, D), 0) // SP
        xs[...] = jnp.where(item < cnt_ref[0], y, 0.0)
        for i in range(IB):
            o_ref[i] = xs[pl.ds(i * SP, seq), :].astype(BF16)

    (output,) = call(
        out_body,
        (total_steps,),
        [item_counts, h_all, y_part, y_got, down_b],
        [smem(), rowD, rowD, rowD, whole((1, D))],
        [sds(tokens.shape, BF16)],
        [tok_spec],
        [pltpu.VMEM((BR, D), F32)],
        after=(grad_tokens,),
    )

    small = jnp.concatenate(
        [
            jnp.sum(qkv_sums, axis=(0, 1))[: W],
            jnp.sum(qkv_sums, axis=(0, 1))[2 * W :],
            jnp.sum(back2_sums, axis=0).reshape(-1),
            jnp.concatenate([s.reshape(-1) for s in up_sums]),
            jnp.sum(dy_sums, axis=(0, 1)),
            jnp.sum(back1_sums, axis=0).reshape(-1),
        ]
    )
    gds, gus = lax.psum((gds, gus), "dp")
    gqkv, go, small = lax.psum((gqkv, go, small), "dp")
    grad_down = jnp.concatenate(gds, axis=0)
    grad_up = jnp.concatenate(gus, axis=1)
    grad_qkv = jnp.transpose(gqkv, (1, 0, 2))
    at = 0

    def take(n):
        nonlocal at
        at += n
        return small[at - n : at]

    grad_qv_bias = take(2 * W).reshape(2, W)
    gain2, shift2, grad_out_bias = take(D), take(D), take(D)
    grad_up_bias = take(FL)
    grad_down_bias = take(D)
    gain1, shift1 = take(D), take(D)
    return (
        output,
        grad_tokens,
        grad_qkv,
        grad_qv_bias,
        go,
        grad_out_bias,
        grad_up,
        grad_up_bias,
        grad_down,
        grad_down_bias,
        jnp.stack([gain1, gain2]),
        jnp.stack([shift1, shift2]),
    )


def solution(mesh):
    return jax.shard_map(
        on_device,
        mesh=mesh,
        in_specs=(
            P("dp", None, None),
            P("dp", None, None),
            P("dp"),
            P("dp"),
            P(None, None, "tensor"),
            P(None, "tensor"),
            P("tensor", None),
            P(),
            P(None, "tensor"),
            P("tensor"),
            P("tensor", None),
            P(),
            P(),
            P(),
        ),
        out_specs=(
            P("dp", None, None),
            P("dp", None, None),
            P(None, None, "tensor"),
            P(None, "tensor"),
            P("tensor", None),
            P(),
            P(None, "tensor"),
            P("tensor"),
            P("tensor", None),
            P(),
            P(),
            P(),
        ),
        check_vma=False,
    )
```

time: 733 us -> 595 us (0.81)
  Pallas kernels: 0 us -> 138 us
  matrix products: 121 us -> 0 us
  local copies, waits for them, and re-layouts: 119 us -> 31 us
  other arithmetic: 43.5 us -> 9.2 us
  waiting for transfers between devices: 346 us -> 319 us
    pallas_call x0 -> x15, Pallas kernels: none -> 138 us  [call(): pl.pallas_call(kernel, grid=grid, in_specs=list(in_specs) + [anywhere()]...]
    dot_general x18 -> x0, matrix products: 121 us -> none  [the longest x1 25.3 us: on_device(): jnp.dot(second_low, w_up, preferred_element_type=jnp.float32) + up_bias]
    convert_element_type x8 -> x0, local copies, waits for them, and re-layouts: 32.6 us -> none  [the longest x2 9.6 us: on_device(): inputs = tokens.reshape(total_rows, model_width).astype(jnp.float32)]
    psum x4 -> x1, waiting for transfers between devices: 346 us -> 318 us  [on_device(): gqkv, go, small = lax.psum((gqkv, go, small), 'dp')]
    reduce_sum x9 -> x4, other arithmetic: 26.4 us -> 0.09 us  [the longest x1 0.03 us: on_device(): jnp.sum(qkv_sums, axis=(0, 1))[:W]]
    another operation x13 -> x4, local copies, waits for them, and re-layouts: 25.3 us -> 0.01 us  [the longest x2 0.01 us: on_device(): jnp.stack([gain1, gain2])]
    convert_element_type x6 -> x0, other arithmetic: 15.7 us -> none  [the longest x1 5.49 us: on_device(): grad_tokens = grad_inputs.astype(jnp.bfloat16).reshape(tokens.shape)]
    squeeze x2 -> x0, local copies, waits for them, and re-layouts: 9.59 us -> none  [the longest x1 4.79 us: on_device(): projected[:, 0] + qv_bias[0]]
  transfers between devices with their start and end apart: 4 -> 6, of which waited for: 4 -> 1; matrix products, arithmetic and copies ran while one was open for 10% -> 2% of each run, Pallas kernels for 0% -> 6%
where the time goes in v1:
time: 595 us
  waiting for transfers between devices  319 us (54%)
  Pallas kernels  138 us (23%)
  blocking collectives  81.3 us (14%)
  local copies, waits for them, and re-layouts  31 us (5%)
  between operations  15.1 us (3%)
  other arithmetic  9.2 us (2%)
    psum x1, waiting for transfers between devices, on_device(): gqkv, go, small = lax.psum((gqkv, go, small), 'dp')  318 us
    pallas_call x15, Pallas kernels, call(): pl.pallas_call(kernel, grid=grid, in_specs=list(in_specs) + [anywhere()]...  138 us
    psum x1, blocking collectives, on_device(): gqkv, go, small = lax.psum((gqkv, go, small), 'dp')  81.3 us
    unnamed x69, local copies, waits for them, and re-layouts  24 us
  transfers between devices with their start and end apart: 6, of which 1 were waited for; matrix products, arithmetic and copies ran while one was open for 2% of the time, Pallas kernels for 6%

profile of v1, /device:TPU:0, one launch (start us, length us, event | category | flops | bytes accessed | tf_op | source)
XLA Modules:
  0.0 594.9 jit_solution(17684930464090534957)
XLA Ops:
  7.2 3.6 copy.58.refs_1_.refs_0_
  12.4 2.2 copy.55.refs_2_.refs_3_
  15.2 8.9 %shard_map.229 = (f32[768,768]{1,0:T(8,128)}, bf16[1536,768]{1,0:T(8,128)(2,1)}, bf16[1536,1152]{1,0:T(8,128)(2,1)}, bf16[8,6,192,192]{3,2,1,0:T(8,128)(2,1)}, bf16[1536,384]{1,0:T(8,128)(2,1)}) custom-call(s32[8]{0:T(128)} %refs_0_.7, bf16[8,185,768]{2,1,0:T(8,128)(2,1)} %copy.58.refs_1_.refs_0_, bf16[768,1152]{1,0:T(8,128)(2,1)} %copy.55.refs_2_.refs_3_, ...), custom_call_target="tpu_custom_call" | custom-call | flops 1811939328 | bytes 17619488 | tf_op jit(solution)/shard_map/pallas_call | solution.py:39
  24.6 9.0 %shard_map.230 = (f32[768,768]{1,0:T(8,128)}, bf16[1536,768]{1,0:T(8,128)(2,1)}, bf16[1536,1152]{1,0:T(8,128)(2,1)}, bf16[8,6,192,192]{3,2,1,0:T(8,128)(2,1)}, bf16[1536,384]{1,0:T(8,128)(2,1)}) custom-call(s32[8]{0:T(128)} %refs_0_.7, ...), custom_call_target="tpu_custom_call", output_to_operand_aliasing={{1}: (7, {}), {2}: (8, {}), {3}: (9, {}), {4}: (10, {})} | custom-call | flops 1811939328 | bytes 28236320 | tf_op jit(solution)/shard_map/pallas_call | solution.py:39
  39.0 5.0 shard_map.231
  45.4 5.0 shard_map.232
  50.4 9.9 %shard_map.233 = (f32[384,768]{1,0:T(8,128)}, f32[768,384]{1,0:T(8,128)}, f32[1,384]{1,0:T(1,128)}, bf16[1536,1536]{1,0:T(8,128)(2,1)}, bf16[1536,1536]{1,0:T(8,128)(2,1)}) custom-call(bf16[1536,768]{1,0:T(8,128)(2,1)} %get-tuple-element.73.refs_0_, bf16[768,1536]{1,0:T(8,128)(2,1)} %get-tuple-element.74.refs_1_, ...), custom_call_target="tpu_custom_call" | custom-call | flops 3623878656 | bytes 23600640 | tf_op jit(solution)/shard_map/pallas_call | solution.py:39
  60.3 10.1 %shard_map.234 = (f32[384,768]{1,0:T(8,128)}, f32[768,384]{1,0:T(8,128)}, f32[1,384]{1,0:T(1,128)}, bf16[1536,1536]{1,0:T(8,128)(2,1)}, bf16[1536,1536]{1,0:T(8,128)(2,1)}) custom-call(bf16[1536,768]{1,0:T(8,128)(2,1)} %get-tuple-element.73.refs_0_, bf16[768,1536]{1,0:T(8,128)(2,1)} %get-tuple-element.74.refs_1_, ...), custom_call_target="tpu_custom_call", output_to_operand_aliasing={{3}: (6, {}), {4}: (7, {})} | custom-call | flops 3623878656 | bytes 33037824 | tf_op jit(solution)/shard_map/pallas_call | solution.py:39
  70.4 9.9 %shard_map.235 = (f32[384,768]{1,0:T(8,128)}, f32[768,384]{1,0:T(8,128)}, f32[1,384]{1,0:T(1,128)}, bf16[1536,1536]{1,0:T(8,128)(2,1)}, bf16[1536,1536]{1,0:T(8,128)(2,1)}) custom-call(bf16[1536,768]{1,0:T(8,128)(2,1)} %get-tuple-element.73.refs_0_, bf16[768,1536]{1,0:T(8,128)(2,1)} %get-tuple-element.74.refs_1_, ...), custom_call_target="tpu_custom_call", output_to_operand_aliasing={{3}: (6, {}), {4}: (7, {})} | custom-call | flops 3623878656 | bytes 33037824 | tf_op jit(solution)/shard_map/pallas_call | solution.py:39
  80.3 9.9 %shard_map.236 = (f32[384,768]{1,0:T(8,128)}, f32[768,384]{1,0:T(8,128)}, f32[1,384]{1,0:T(1,128)}, bf16[1536,1536]{1,0:T(8,128)(2,1)}, bf16[1536,1536]{1,0:T(8,128)(2,1)}) custom-call(bf16[1536,768]{1,0:T(8,128)(2,1)} %get-tuple-element.73.refs_0_, bf16[768,1536]{1,0:T(8,128)(2,1)} %get-tuple-element.74.refs_1_, ...), custom_call_target="tpu_custom_call", output_to_operand_aliasing={{3}: (6, {}), {4}: (7, {})} | custom-call | flops 3623878656 | bytes 33037824 | tf_op jit(solution)/shard_map/pallas_call | solution.py:39
  90.3 8.3 %shard_map.237.refs_2_.refs_0_ = f32[1536,768]{1,0:T(8,128)} custom-call(bf16[1536,1536]{1,0:T(8,128)(2,1)} %get-tuple-element.83.refs_0_, bf16[768,1536]{1,0:T(8,128)(2,1)} %refs_1_.6), custom_call_target="tpu_custom_call" | custom-call | flops 3623878656 | bytes 11796480 | tf_op jit(solution)/shard_map/pallas_call | solution.py:39
  99.0 8.1 %shard_map.238.refs_7_.refs_2_ = f32[1536,768]{1,0:T(8,128)} custom-call(bf16[1536,1536]{1,0:T(8,128)(2,1)} %get-tuple-element.82.refs_0_, bf16[1536,768]{1,0:T(8,128)(2,1)} %refs_1_.7, f32[1536,768]{1,0:T(8,128)} %shard_map.237.refs_2_.refs_0_), custom_call_target="tpu_custom_call" | custom-call | flops 3623878656 | bytes 11796480 | tf_op jit(solution)/shard_map/pallas_call | solution.py:39
  107.1 2.2 copy-done.2
  109.3 11.9 %shard_map.239 = (bf16[1536,768]{1,0:T(8,128)(2,1)}, bf16[1536,384]{1,0:T(8,128)(2,1)}, f32[384,768]{1,0:T(8,128)}, f32[4,3,768]{2,1,0:T(4,128)}) custom-call(f32[1536,768]{1,0:T(8,128)} %shard_map.237.refs_2_.refs_0_, f32[1536,768]{1,0:T(8,128)} %copy-done.2, bf16[1536,768]{1,0:T(8,128)(2,1)} %get-tuple-element.72.refs_2_.refs_1_, ...), custom_call_target="tpu_custom_call" | custom-call | flops 1811939328 | bytes 20683776 | tf_op jit(solution)/shard_map/pallas_call | solution.py:39
  121.3 17.8 %shard_map.240 = (bf16[1536,1152]{1,0:T(8,128)(2,1)}, f32[1536,768]{1,0:T(8,128)}, f32[4,1,1152]{2,1,0:T(1,128)}) custom-call(bf16[8,6,192,192]{3,2,1,0:T(8,128)(2,1)} %get-tuple-element.84.refs_0_, bf16[1536,1152]{1,0:T(8,128)(2,1)} %get-tuple-element.85.refs_1_, bf16[1536,384]{1,0:T(8,128)(2,1)} %get-tuple-element.87.refs_2_, ...), custom_call_target="tpu_custom_call" | custom-call | flops 2717908992 | bytes 18302976 | tf_op jit(solution)/shard_map/pallas_call | solution.py:39
  139.1 8.2 %shard_map.241.refs_5_ = f32[3,768,384]{2,1,0:T(8,128)} custom-call(bf16[1536,768]{1,0:T(8,128)(2,1)} %get-tuple-element.90.refs_0_, bf16[1536,1152]{1,0:T(8,128)(2,1)} %get-tuple-element.91.refs_1_, f32[1536,768]{1,0:T(8,128)} %get-tuple-element.88.refs_2_.refs_1_), custom_call_target="tpu_custom_call" | custom-call | flops 2717908992 | bytes 9437184 | tf_op jit(solution)/shard_map/pallas_call | solution.py:39
  149.5 8.7 %shard_map.242 = (bf16[8,185,768]{2,1,0:T(8,128)(2,1)}, f32[4,2,768]{2,1,0:T(2,128)}) custom-call(bf16[8,185,768]{2,1,0:T(8,128)(2,1)} %copy.58.refs_1_.refs_0_, f32[1536,768]{1,0:T(8,128)} %get-tuple-element.88.refs_2_.refs_1_, f32[1536,768]{1,0:T(8,128)} %copy-done.1, bf16[1536,768]{1,0:T(8,128)(2,1)} %get-tuple-element.89.refs_3_, ...), custom_call_target="tpu_custom_call" | custom-call | bytes 16370688 | tf_op jit(solution)/shard_map/pallas_call | solution.py:39
  160.4 81.3 %psum.78 = f32[6912]{0:T(1024)S(1)} all-reduce(f32[6912]{0:T(1024)S(1)} %constant_dynamic-update-slice_fusion), channel_id=1, replica_groups=mesh['dp'=16,'tensor'=2] {'dp'}, use_global_device_ids=true, to_apply=%region_5.0 | all-reduce | flops 6912 | bytes 55296 | tf_op jit(solution)/shard_map/psum | solution.py:532
  243.5 2.6 copy.63
  246.1 6.9 %shard_map.243 = bf16[8,185,768]{2,1,0:T(8,128)(2,1)} custom-call(s32[1]{0:T(128)S(6)} %copy.98.refs_0_, bf16[1536,768]{1,0:T(8,128)(2,1)} %get-tuple-element.72.refs_2_.refs_1_, f32[1536,768]{1,0:T(8,128)} %shard_map.238.refs_7_.refs_2_, f32[1536,768]{1,0:T(8,128)} %collective-permute-done.2.refs_3_, f32[1,768]{1,0:T(1,128)} %reshape.70.refs_4_, ...), custom_call_target="tpu_custom_call" | custom-call | bytes 14072836 | tf_op jit(solution)/shard_map/pallas_call | solution.py:39
  253.0 4.3 copy.62
  258.5 318.4 %all-reduce.3.cloned.1.call-done = (f32[768,3,384]{2,0,1:T(8,128)}, f32[384,768]{1,0:T(8,128)}, f32[768,384]{1,0:T(8,128)}, f32[768,384]{1,0:T(8,128)}, f32[768,...) async-done(((f32[768,3,384]{2,0,1:T(8,128)}, f32[384,768]{1,0:T(8,128)}, ...) | async-done | bytes 14155792 | tf_op jit(solution)/shard_map/psum | solution.py:532
  576.9 5.0 pad_maximum_fusion.1
  582.0 2.8 pad_maximum_fusion
  (106 shorter events, 19.7 us)
Async XLA Ops:
  7.2 3.6 copy-start.22
  7.2 4.3 copy-start.7
  12.4 2.2 copy-start.18
  12.4 2.2 copy-start.19
  24.1 13.4 %collective-permute-start.1 = (f32[768,768]{1,0:T(8,128)}, f32[768,768]{1,0:T(8,128)S(1)}, u32[]{:S(2)}, u32[]{:S(2)}) collective-permute-start(f32[768,768]{1,0:T(8,128)} %get-tuple-element.66.refs_3_), channel_id=1, source_target_pairs={{0,1},{1,0},{2,3},{3,2},{4,5},{5,4},{6,7},{7,6},{8,9},{9,8},{10,11... | collective-permute-start | bytes 7077896 | tf_op jit(solution)/shard_map/ppermute | solution.py:206
  24.6 9.8 %copy-start.6 = (bf16[8,185,768]{2,0,1:T(8,128)(2,1)S(1)}, bf16[8,185,768]{2,0,1:T(8,128)(2,1)}, u32[]{:S(2)}) copy-start(bf16[8,185,768]{2,0,1:T(8,128)(2,1)} %param.15) | copy-start | bytes 6819844
  33.6 2.7 copy-start.20
  33.7 3.2 copy-start.17
  33.7 10.3 %collective-permute-start = (f32[768,768]{1,0:T(8,128)}, f32[768,768]{1,0:T(8,128)S(1)}, u32[]{:S(2)}, u32[]{:S(2)}) collective-permute-start(f32[768,768]{1,0:T(8,128)} %get-tuple-element.65.refs_3_), channel_id=1, source_target_pairs={{0,1},{1,0},{2,3},{3,2},{4,5},{5,4},{6,7},{7,6},{8,9},{9,8},{10,11... | collective-permute-start | bytes 7077896 | tf_op jit(solution)/shard_map/ppermute | solution.py:206
  98.6 8.6 %collective-permute-start.3 = (f32[1536,768]{1,0:T(8,128)}, f32[1536,768]{1,0:T(8,128)S(1)}, u32[]{:S(2)}, u32[]{:S(2)}) collective-permute-start(f32[1536,768]{1,0:T(8,128)} %shard_map.237.refs_2_.refs_0_), channel_id=1, source_target_pairs={{0,1},{1,0},{2,3},{3,2},{4,5},{5,4},{6,7},{7,6},{8,9},{9,8},{10,11... | collective-permute-start | bytes 14155784 | tf_op jit(solution)/shard_map/ppermute | solution.py:206
  107.1 2.2 copy-start.2
  139.0 8.2 %collective-permute-start.4 = (f32[1536,768]{1,0:T(8,128)}, f32[1536,768]{1,0:T(8,128)S(1)}, u32[]{:S(2)}, u32[]{:S(2)}) collective-permute-start(f32[1536,768]{1,0:T(8,128)} %get-tuple-element.88.refs_2_.refs_1_), channel_id=1, source_target_pairs={{0,1},{1,0},{2,3},{3,2},{4,5},{5,4},{6,7},{7,6},{8,9},{9,8},{10,11... | collective-permute-start | bytes 14155784 | tf_op jit(solution)/shard_map/ppermute | solution.py:206
  147.3 2.2 copy-start.1
  158.1 418.8 %all-reduce.3.cloned.1.call-start = ((), (), s32[]{:S(2)}) async-start(), calls=%async_computation | async-start | bytes 28311552 | tf_op jit(solution)/shard_map/psum | solution.py:532
  158.2 1.9 copy-start.14
  158.3 2.1 copy-start.15
  158.3 85.2 %copy-start = (bf16[8,185,768]{2,1,0:T(8,128)(2,1)S(1)}, bf16[8,185,768]{2,1,0:T(8,128)(2,1)}, u32[]{:S(2)}) copy-start(bf16[8,185,768]{2,1,0:T(8,128)(2,1)} %get-tuple-element.123.refs_5_) | copy-start | bytes 6819844
  158.9 87.3 %collective-permute-start.2 = (f32[1536,768]{1,0:T(8,128)}, f32[1536,768]{1,0:T(8,128)}, u32[]{:S(2)}, u32[]{:S(2)}) collective-permute-start(f32[1536,768]{1,0:T(8,128)} %shard_map.238.refs_7_.refs_2_), channel_id=1, source_target_pairs={{0,1},{1,0},{2,3},{3,2},{4,5},{5,4},{6,7},{7,6},{8,9},{9,8},{10,11... | collective-permute-start | bytes 14155784 | tf_op jit(solution)/shard_map/ppermute | solution.py:206
  576.9 5.0 copy-start.8
  576.9 5.0 copy-start.9
  576.9 5.0 copy-start.10
  576.9 5.0 copy-start.11
  581.9 3.0 copy-start.3
  584.9 2.1 copy-start.12
  (9 other events, 15.1 us)
Sparse Core Ops, SparseCore 0:
  166.0 410.9 all-reduce.2
